TPU v7x, 32 devices: a whole 2x2x4 slice. The times are simulated.
32 devices in a mesh: wide: 16 (over z, x, core), narrow: 2 (over y).
Axes of the slice: x: 2, y: 2, z: 4, core: 2. Of those that a mesh axis runs over, the one named last changes fastest.
Arguments:
- amplitudes: bfloat16 [2048, 2048], P(('wide', 'narrow')), may hold values from -6 to 6
- amp_mask: int32 [32, 32], replicated, may hold values from 0 to 1, as said below
- integrals: bfloat16 [2048, 8192], P('narrow', 'wide'), may hold values from -0.59765625 to 0.59765625
- int_mask: int32 [32, 128], replicated, may hold values from 0 to 1, as said below
- owner: int32 [128], replicated, may hold values from 0 to 127, each once
- occ_energy: float32 [2048], P('narrow'), may hold values from -3 to -0.5
- vir_energy: float32 [8192], replicated, may hold values from 1 to 8
Outputs:
- update: bfloat16 [2048, 8192], P('narrow', 'wide')
Inputs may be any that keep to these rules, and one draw needn't show every extreme that they name: `amp_mask`: 1 marks a pair of tiles within the screening distance, 0 one outside it. `int_mask`: 1 marks a pair of tiles within the screening distance, 0 one outside it. A permutation of the 128 tiles; columns 64 * s to 64 * s + 63 of integrals and update belong to tile owner[s].
All inputs are finite; a program needn't handle non-finite values.
Results may differ from a plain program's by a relative error of at most 0.001.
Values may be sent and summed in bfloat16 or wider, within the bound.
A program may use at most 64 MiB of HBM per device.

v0:
```python
import jax
import jax.numpy as jnp
from jax import lax
from jax.sharding import PartitionSpec as P

TILE = 64


def contract_rows(summed, rows_in, int_part):
    return summed + lax.dot_general(
        rows_in, int_part, (((0,), (0,)), ((), ())), preferred_element_type=jnp.float32
    )


def contract_all(amp_full, int_full, starting):
    k_total = amp_full.shape[0]
    block_rows = min(512, k_total)
    summed = starting
    for first_row in range(0, k_total, block_rows):
        summed = contract_rows(
            summed,
            amp_full[first_row : first_row + block_rows],
            int_full[first_row : first_row + block_rows],
        )
    return summed


def shards(amplitudes, amp_mask, integrals, int_mask, owner, occ_energy, vir_energy):
    tile_width = TILE
    narrow_count = lax.axis_size("narrow")
    wide_index = lax.axis_index("wide")
    narrow_index = lax.axis_index("narrow")
    src_rows = amplitudes.shape[0]
    occ_all = amplitudes.shape[1]
    occ_here = occ_energy.shape[0]
    vir_here = integrals.shape[1]
    first_src = (wide_index * narrow_count + narrow_index) * src_rows
    src_tiles = (first_src + jnp.arange(src_rows, dtype=jnp.int32)) // tile_width
    src_mask = jnp.take(amp_mask, src_tiles, axis=0)
    src_wide = jnp.broadcast_to(
        src_mask[:, :, None], (src_rows, occ_all // tile_width, tile_width)
    ).reshape(src_rows, occ_all)
    masked = jnp.where(src_wide == 1, amplitudes, jnp.zeros((), amplitudes.dtype))
    vir_tiles_here = vir_here // tile_width
    slot_ids = wide_index * vir_tiles_here + jnp.arange(vir_tiles_here, dtype=jnp.int32)
    tile_ids = jnp.take(owner, slot_ids)
    vir_mask = jnp.take(int_mask, tile_ids, axis=1)
    int_rows = integrals.shape[0]
    row_tiles = int_rows // tile_width
    local_mask = lax.dynamic_slice_in_dim(vir_mask, narrow_index * row_tiles, row_tiles, 0)
    local_wide = jnp.broadcast_to(
        local_mask[:, None, :, None], (row_tiles, tile_width, vir_tiles_here, tile_width)
    ).reshape(int_rows, vir_here)
    int_masked = jnp.where(local_wide == 1, integrals, jnp.zeros((), integrals.dtype))
    int_full = lax.all_gather(int_masked, "narrow", axis=0, tiled=True)
    starting = jnp.zeros((occ_here, vir_here), jnp.float32)
    regrouped = lax.all_to_all(masked, "narrow", split_axis=1, concat_axis=0, tiled=True)
    amp_full = lax.all_gather(regrouped, "wide", axis=0, tiled=True)
    ladder = contract_all(amp_full, int_full, starting)
    vir_energy_here = jnp.take(vir_energy.reshape(-1, tile_width), tile_ids, axis=0).reshape(
        vir_here
    )
    denominator = vir_energy_here[None, :] - occ_energy[:, None]
    return (ladder / denominator).astype(jnp.bfloat16)


def solution(mesh):
    return jax.shard_map(
        shards,
        mesh=mesh,
        in_specs=(
            P(("wide", "narrow"), None),
            P(),
            P("narrow", "wide"),
            P(),
            P(),
            P("narrow"),
            P(),
        ),
        out_specs=P("narrow", "wide"),
        check_vma=False,
    )
```

profile of v0, /device:TPU:5, one launch (start us, length us, event | category | flops | bytes accessed | tf_op | source)
XLA Modules:
  0.0 114.1 jit_solution(16086881813039988897)
XLA Ops:
  6.5 0.0 copy-start
  6.6 1.4 %gather_fusion.1 = s32[8]{0:T(128)S(1)} fusion(s32[128]{0:T(128)} %param.11, s32[1024]{0:T(1024)S(1)} %pad_clamp_fusion.1), kind=kCustom, calls=%fused_computation.1 | custom fusion | bytes 96 | tf_op jit(solution)/shard_map/jit(_take)/gather | solution.py:46
  8.0 0.8 copy.16
  8.8 0.6 gather_fusion.2
  9.4 0.1 broadcast_select_fusion.2
  9.4 0.1 fusion.11
  9.5 0.1 copy.17
  9.6 0.3 broadcast_in_dim.59
  10.0 1.4 %eq.25 = pred[1024,512]{1,0:T(8,128)(4,1)S(1)} reshape(pred[16,64,8,64]{3,2,1,0:T(8,128)(4,1)S(1)} %broadcast_in_dim.59) | data formatting | bytes 1048576 | tf_op jit(solution)/shard_map/eq | solution.py:54
  11.4 0.0 copy-start.2
  11.4 1.1 broadcast_select_fusion
  12.5 0.0 all-gather.5.cloned.1.call-update
  12.5 0.0 all-gather.3.cloned.1.call-start
  12.6 0.0 copy-done
  12.6 0.6 gather_fusion
  13.2 0.1 select_compare_fusion
  13.3 0.3 broadcast_in_dim.55
  13.7 0.5 eq.22
  14.2 5.7 %all_to_all.19 = bf16[64,2,1024]{2,0,1:T(8,128)(2,1)} all-to-all(bf16[64,2,1024]{2,0,1:T(8,128)(2,1)S(1)} %bitcast.23), channel_id=1, replica_groups=mesh['wide'=16,'narrow'=2] {'narrow'}, dimensions={1} | all-to-all | bytes 524288 | tf_op jit(solution)/shard_map/all_to_all | solution.py:57
  20.0 0.0 all-gather.3.cloned.1.call-update
  20.0 0.1 reshape.162
  20.1 0.6 gather_fusion.3
  20.6 0.1 broadcast_select_fusion.3
  20.7 0.1 select_n.135
  20.8 25.3 %all-gather.5.cloned.1.call-done = bf16[2048,512]{1,0:T(8,128)(2,1)} async-done(((bf16[1024,512]{1,0:T(8,128)(2,1)}), bf16[2048,512]{1,0:T(8,128)(2,1)}) %all-gather.5.cloned.1.call-update) | async-done | bytes 2097168 | tf_op jit(solution)/shard_map/all_gather | solution.py:55
  46.1 54.2 %all-gather.3.cloned.1.call-done = bf16[2048,1024]{1,0:T(8,128)(2,1)} async-done(((bf16[128,1024]{1,0:T(8,128)(2,1)}), bf16[2048,1024]{1,0:T(8,128)(2,1)}) %all-gather.3.cloned.1.call-update) | async-done | bytes 4194320 | tf_op jit(solution)/shard_map/all_gather | solution.py:58
  100.3 2.3 %fusion.1 = f32[1024,512]{1,0:T(8,128)S(1)} fusion(bf16[2048,1024]{1,0:T(8,128)(2,1)} %all-gather.3.cloned.1.call-done, bf16[2048,512]{1,0:T(8,128)(2,1)} %all-gather.5.cloned.1.call-done), kind=kOutput, calls=%fused_computation.6 | convolution fusion | flops 536870912 | bytes 3670016 | tf_op jit(solution)/shard_map/dot_general | solution.py:10
  102.6 0.0 copy-done.5
  102.6 2.0 %fusion.3 = f32[1024,512]{1,0:T(8,128)S(1)} fusion(bf16[2048,1024]{1,0:T(8,128)(2,1)} %all-gather.3.cloned.1.call-done, bf16[2048,512]{1,0:T(8,128)(2,1)S(1)} %copy-done.5), kind=kOutput, calls=%fused_computation.8 | convolution fusion | flops 536870912 | bytes 3670016 | tf_op jit(solution)/shard_map/dot_general | solution.py:10
  104.6 0.0 copy-start.6
  104.6 0.8 fusion.5
  105.4 2.0 %divide_convert_fusion = bf16[1024,512]{1,0:T(8,128)(2,1)} fusion(f32[1024,512]{1,0:T(8,128)S(1)} %fusion.1, f32[1024,512]{1,0:T(8,128)S(1)} %fusion.5, f32[1024,512]{1,0:T(8,128)S(1)} %fusion.3, bf16[2048,1024]{1,0:T(8,128)(2,1)S(1)} %copy-done.4, f32[1024]{0:T(1024)S(1)} %copy-done.6, f32[512]{0:T(512)S(1)} %select_n.135, bf16[2048,512]{1,0:T(8,128)(2,1)S(1)} %copy-done.5), kind=kOutput, calls=%fused_computation.4 | convolution fusion | flops 540016640 | bytes 8919040 | tf_op jit(solution)/shard_map/dot_general | solution.py:10
  (20 shorter events, 0.1 us)
Async XLA Ops:
  6.5 6.1 %copy-start = (s32[32,32]{1,0:T(8,128)S(1)}, s32[32,32]{1,0:T(8,128)}, u32[]{:S(2)}) copy-start(s32[32,32]{1,0:T(8,128)} %param.8) | copy-start | bytes 12292
  6.5 4.8 %copy-start.1 = (bf16[1024,512]{1,0:T(8,128)(2,1)S(1)}, bf16[1024,512]{1,0:T(8,128)(2,1)}, u32[]{:S(2)}) copy-start(bf16[1024,512]{1,0:T(8,128)(2,1)} %param.9) | copy-start | bytes 3145732
  6.5 39.6 %all-gather.5.cloned.1.call-start = ((), (), s32[]{:S(2)}) async-start(), calls=%async_computation.2 | async-start | bytes 3145728 | tf_op jit(solution)/shard_map/all_gather | solution.py:55
  11.4 2.8 %copy-start.2 = (bf16[64,2048]{1,0:T(8,128)(2,1)S(1)}, bf16[64,2048]{1,0:T(8,128)(2,1)}, u32[]{:S(2)}) copy-start(bf16[64,2048]{1,0:T(8,128)(2,1)} %param.7) | copy-start | bytes 786436
  12.5 7.5 %copy-start.3 = (f32[8192]{0:T(1024)S(1)}, f32[8192]{0:T(1024)}, u32[]{:S(2)}) copy-start(f32[8192]{0:T(1024)} %param.13) | copy-start | bytes 98308
  12.5 87.8 %all-gather.3.cloned.1.call-start = ((), (), s32[]{:S(2)}) async-start(), calls=%async_computation.1 | async-start | bytes 4456448 | tf_op jit(solution)/shard_map/all_gather | solution.py:58
  46.1 56.5 %copy-start.5 = (bf16[2048,512]{1,0:T(8,128)(2,1)S(1)}, bf16[2048,512]{1,0:T(8,128)(2,1)}, u32[]{:S(2)}) copy-start(bf16[2048,512]{1,0:T(8,128)(2,1)} %all-gather.5.cloned.1.call-done) | copy-start | bytes 6291460
  100.3 4.2 %copy-start.4 = (bf16[2048,1024]{1,0:T(8,128)(2,1)S(1)}, bf16[2048,1024]{1,0:T(8,128)(2,1)}, u32[]{:S(2)}) copy-start(bf16[2048,1024]{1,0:T(8,128)(2,1)} %all-gather.3.cloned.1.call-done) | copy-start | bytes 12582916
  104.6 0.8 copy-start.6
Sparse Core Ops, SparseCore 0:
  12.6 33.4 all-gather.4
  48.3 52.0 all-gather.2
where the time goes:
time: 116 us; the launch traced here: 114 us
  waiting for transfers between devices  79.6 us (69%)
  between operations  13.6 us (12%)
  matrix products  6.94 us (6%)
  local copies, waits for them, and re-layouts  6.78 us (6%)
  blocking collectives  5.75 us (5%)
  other arithmetic  1.48 us (1%)
    all_gather x1, waiting for transfers between devices, shards(): amp_full = lax.all_gather(regrouped, 'wide', axis=0, tiled=True)  54.2 us
    all_gather x1, waiting for transfers between devices, shards(): int_full = lax.all_gather(int_masked, 'narrow', axis=0, tiled=True)  25.3 us
    dot_general x4, matrix products, contract_rows(): lax.dot_general(rows_in, int_part, (((0,), (0,)), ((), ())), preferred_el...  6.94 us
    all_to_all x1, blocking collectives, shards(): lax.all_to_all(masked, 'narrow', split_axis=1, concat_axis=0, tiled=True)  5.75 us
  transfers between devices with their start and end apart: 2, of which 2 were waited for; matrix products, arithmetic and copies ran while one was open for 2% of the time, Pallas kernels for 0%

commit v1 on v0

--- a/solution.py
+++ b/solution.py
@@ -1,6 +1,10 @@
+import functools
+
 import jax
 import jax.numpy as jnp
 from jax import lax
+from jax.experimental import pallas as pl
+from jax.experimental.pallas import tpu as pltpu
 from jax.sharding import PartitionSpec as P
 
 TILE = 64
@@ -64,19 +68,439 @@
     return (ladder / denominator).astype(jnp.bfloat16)
 
 
+MESH = pl.DeviceIdType.MESH
+LANES = 128
+
+
+def lookup(table, z, y):
+    value = jnp.int32(table[0][0])
+    for zz in range(len(table)):
+        for yy in range(2):
+            value = jnp.where((z == zz) & (y == yy), jnp.int32(table[zz][yy]), value)
+    return value
+
+
+def schedule(z_count):
+    half = z_count // 2
+    orders, sends = [], []
+    for z in range(z_count):
+        row, send = [], []
+        for y in range(2):
+            remote = sorted(range((1 - y) * half, (2 - y) * half), key=lambda g: abs(g - z))
+            near = sorted((g for g in range(z_count) if g != remote[-1]), key=lambda g: abs(g - z))
+            row.append(near + [remote[-1]])
+            send.append(sorted(range(y * half, (y + 1) * half), key=lambda g: abs(g - z)))
+        orders.append(row)
+        sends.append(send)
+    return orders, sends
+
+
+def ladder_kernel(
+    z_count,
+    amp_hbm,
+    int_hbm,
+    amask_ref,
+    imask_ref,
+    owner_ref,
+    occ_ref,
+    vir_ref,
+    out_hbm,
+    amp_scr,
+    int_scr,
+    acc,
+    recip,
+    amask,
+    imask,
+    out_scr,
+    occ_cols,
+    own_sem,
+    ycross_send,
+    int_send,
+    int_recv,
+    send_sem,
+    recv_sem,
+    out_sem,
+):
+    w = lax.axis_index("wide")
+    y = lax.axis_index("narrow")
+    z, x, c = w // 4, (w // 2) % 2, w % 2
+    rows = amp_hbm.shape[0]
+    occ_here, vir_here = acc.shape
+    group = int_scr.shape[0] // z_count
+    half_groups = z_count // 2
+    orders, sends = schedule(z_count)
+
+    def wide_id(zz, xx, cc):
+        return zz * 4 + xx * 2 + cc
+
+    y_peer = (w, 1 - y)
+    x_peer = (wide_id(z, 1 - x, c), y)
+    c_peer = (wide_id(z, x, 1 - c), y)
+    r_peer = (w + 4, y)
+    l_peer = (w - 4, y)
+    has_r, has_l = z < z_count - 1, z > 0
+
+    barrier = pltpu.get_barrier_semaphore()
+    for peer in (y_peer, x_peer, c_peer):
+        pl.semaphore_signal(barrier, inc=1, device_id=peer, device_id_type=MESH)
+
+    @pl.when(has_r)
+    def _():
+        pl.semaphore_signal(barrier, inc=1, device_id=r_peer, device_id_type=MESH)
+
+    @pl.when(has_l)
+    def _():
+        pl.semaphore_signal(barrier, inc=1, device_id=l_peer, device_id_type=MESH)
+
+    pl.semaphore_wait(barrier, 3 + jnp.where(has_r, 1, 0) + jnp.where(has_l, 1, 0))
+
+    def block_id(zz, xx, cc, h):
+        return wide_id(zz, xx, cc) * 2 + h
+
+    def block(zz, xx, cc, h):
+        first = pl.multiple_of(block_id(zz, xx, cc, h) * rows, rows)
+        return amp_scr.at[pl.ds(first, rows), :]
+
+    def half_cols(yy):
+        return amp_hbm.at[:, pl.ds(pl.multiple_of(yy * occ_here, LANES), occ_here)]
+
+    RIGHT, LEFT, ACROSS, CORE, CORE2 = range(5)
+    peers = (r_peer, l_peer, x_peer, c_peer, c_peer)
+
+    def copy(kind, zz, xx, h, src=None):
+        there = block(zz, xx, c, h)
+        return pltpu.make_async_remote_copy(
+            src_ref=there if src is None else src,
+            dst_ref=there,
+            send_sem=send_sem.at[kind, zz * 2 + h],
+            recv_sem=recv_sem.at[block_id(zz, xx, c, h)],
+            device_id=peers[kind],
+            device_id_type=MESH,
+        )
+
+    def arrived(zz, xx, cc, h):
+        here = block(zz, xx, cc, h)
+        pltpu.make_async_remote_copy(
+            src_ref=here,
+            dst_ref=here,
+            send_sem=send_sem.at[CORE, zz * 2 + h],
+            recv_sem=recv_sem.at[block_id(zz, xx, cc, h)],
+            device_id=c_peer,
+            device_id_type=MESH,
+        ).wait_recv()
+
+    cross = pltpu.make_async_remote_copy(
+        src_ref=half_cols(1 - y),
+        dst_ref=block(z, x, c, y),
+        send_sem=ycross_send,
+        recv_sem=recv_sem.at[block_id(z, x, c, y)],
+        device_id=y_peer,
+        device_id_type=MESH,
+    )
+    cross.start()
+
+    def spread_own(h, src):
+        @pl.when(has_r)
+        def _():
+            copy(RIGHT, z, x, h, src).start()
+
+        @pl.when(has_l)
+        def _():
+            copy(LEFT, z, x, h, src).start()
+
+        copy(ACROSS, z, x, h, src).start()
+        copy(CORE, z, x, h, src).start()
+
+    spread_own(y, half_cols(y))
+
+    def int_rows(g):
+        return int_scr.at[pl.ds(pl.multiple_of(g * group, group), group), :]
+
+    def int_local(g):
+        first = pl.multiple_of((g - y * half_groups) * group, group)
+        return int_hbm.at[pl.ds(first, group), :]
+
+    def int_copy(g):
+        return pltpu.make_async_remote_copy(
+            src_ref=int_local(g),
+            dst_ref=int_rows(g),
+            send_sem=int_send.at[g],
+            recv_sem=int_recv.at[g],
+            device_id=y_peer,
+            device_id_type=MESH,
+        )
+
+    for i in range(half_groups):
+        int_copy(lookup([[r[i] for r in row] for row in sends], z, y)).start()
+
+    own_copy = pltpu.make_async_copy(half_cols(y), block(z, x, c, y), own_sem.at[0])
+    own_copy.start()
+    held = pltpu.make_async_copy(
+        int_hbm,
+        int_scr.at[
+            pl.ds(pl.multiple_of(y * half_groups * group, group), half_groups * group), :
+        ],
+        own_sem.at[1],
+    )
+    held.start()
+
+    slots = vir_here // TILE
+    lane = lax.broadcasted_iota(jnp.int32, (1, vir_here), 1) // TILE
+    tile_of = jnp.zeros((1, vir_here), jnp.int32)
+    for j in range(slots):
+        tile_of = jnp.where(lane == j, owner_ref[w * slots + j], tile_of)
+    q_tiles = imask_ref.shape[1]
+    pick = lax.broadcasted_iota(jnp.int32, (q_tiles, vir_here), 0) == tile_of
+    imask[...] = jnp.dot(
+        imask_ref[...].astype(jnp.float32).astype(jnp.bfloat16),
+        jnp.where(pick, 1.0, 0.0).astype(jnp.bfloat16),
+        preferred_element_type=jnp.float32,
+    )
+    p_tiles = amask_ref.shape[1]
+    p_tile = y * (occ_here // TILE) + lax.broadcasted_iota(jnp.int32, (p_tiles, occ_here), 1) // TILE
+    pick_p = lax.broadcasted_iota(jnp.int32, (p_tiles, occ_here), 0) == p_tile
+    amask[...] = jnp.dot(
+        amask_ref[...].astype(jnp.float32).astype(jnp.bfloat16),
+        jnp.where(pick_p, 1.0, 0.0).astype(jnp.bfloat16),
+        preferred_element_type=jnp.float32,
+    )
+
+    arrived(z, x, c, 1 - y)
+    spread_own(1 - y, block(z, x, c, 1 - y))
+
+    low = lax.broadcasted_iota(jnp.int32, (1, LANES), 1) < TILE
+
+    def energies(tile, upper):
+        row = vir_ref[pl.ds(tile // 2, 1), :]
+        turned = jnp.concatenate([row[:, TILE:], row[:, :TILE]], axis=1)
+        odd = jnp.full((1, LANES), tile % 2, jnp.int32) == upper
+        return jnp.where(odd, row, turned)
+
+    occ_t = jnp.transpose(occ_ref[...])
+    for j in range(occ_here // LANES):
+        occ_cols[j * LANES : (j + 1) * LANES, :] = jnp.broadcast_to(
+            occ_t[:, j : j + 1], (LANES, LANES)
+        )
+    for j in range(slots // 2):
+        first = energies(owner_ref[w * slots + 2 * j], 0)
+        second = energies(owner_ref[w * slots + 2 * j + 1], 1)
+        vir_row = jnp.where(low, first, second)
+
+        @pl.loop(0, occ_here // LANES)
+        def _(i):
+            at = pl.ds(pl.multiple_of(i * LANES, LANES), LANES)
+            recip[at, j * LANES : (j + 1) * LANES] = 1.0 / (vir_row - occ_cols[at, :])
+
+    step = 256
+
+    def masked_integrals(g):
+        @pl.when(g // half_groups != y)
+        def _():
+            pltpu.make_async_remote_copy(
+                src_ref=int_rows(g),
+                dst_ref=int_rows(g),
+                send_sem=int_send.at[g],
+                recv_sem=int_recv.at[g],
+                device_id=y_peer,
+                device_id_type=MESH,
+            ).wait_recv()
+
+        for t in range(group // TILE):
+            at = pl.ds(pl.multiple_of(g * group + t * TILE, TILE), TILE)
+            row = imask[pl.ds(g * (group // TILE) + t, 1), :].astype(jnp.bfloat16)
+            int_scr[at, :] = int_scr[at, :] * jnp.broadcast_to(row, (TILE, vir_here))
+
+    def multiply(g, first, last):
+        masked_integrals(g)
+
+        @pl.loop(0, occ_here // step)
+        def _(i):
+            cols = pl.ds(pl.multiple_of(i * step, step), step)
+            parts = []
+            for t in range(group // TILE):
+                at = pl.ds(pl.multiple_of(g * group + t * TILE, TILE), TILE)
+                row = amask[pl.ds(g * (group // TILE) + t, 1), cols].astype(jnp.bfloat16)
+                parts.append(amp_scr[at, cols] * jnp.broadcast_to(row, (TILE, step)))
+            left = jnp.concatenate(parts, axis=0)
+            here = pl.ds(pl.multiple_of(g * group, group), group)
+            term = lax.dot_general(
+                left, int_scr[here, :], (((0,), (0,)), ((), ())),
+                preferred_element_type=jnp.float32,
+            )
+            if first:
+                acc[cols, :] = term
+            elif not last:
+                acc[cols, :] += term
+            else:
+                out_scr[cols, :] = ((acc[cols, :] + term) * recip[cols, :]).astype(jnp.bfloat16)
+                pltpu.make_async_copy(
+                    out_scr.at[cols, :], out_hbm.at[cols, :], out_sem.at[i]
+                ).start()
+
+    def on_left(s, act):
+        @pl.when(z - s >= 0)
+        def _():
+            act(z - s)
+
+    def on_right(s, act):
+        @pl.when(z + s <= z_count - 1)
+        def _():
+            act(z + s)
+
+    def x_arrivals(s):
+        for h in (y, 1 - y):
+
+            def act(zz):
+                arrived(zz, 1 - x, c, h)
+                copy(CORE2, zz, 1 - x, h).start()
+
+            if s == 0:
+                act(z)
+            else:
+                on_left(s, act)
+                on_right(s, act)
+
+    for s in range(1, z_count):
+        for h in (y, 1 - y):
+
+            def from_left(zz):
+                arrived(zz, x, c, h)
+
+                @pl.when(has_r)
+                def _():
+                    copy(RIGHT, zz, x, h).start()
+
+                copy(ACROSS, zz, x, h).start()
+                copy(CORE, zz, x, h).start()
+
+            def from_right(zz):
+                arrived(zz, x, c, h)
+
+                @pl.when(has_l)
+                def _():
+                    copy(LEFT, zz, x, h).start()
+
+                copy(ACROSS, zz, x, h).start()
+                copy(CORE, zz, x, h).start()
+
+            on_left(s, from_left)
+            on_right(s, from_right)
+        x_arrivals(s - 1)
+
+    own_copy.wait()
+    held.wait()
+
+    def core_arrivals(g):
+        for xx in range(2):
+            for h in range(2):
+                arrived(g, xx, 1 - c, h)
+
+    group_at = [lookup([[r[i] for r in row] for row in orders], z, y) for i in range(z_count)]
+    for i in range(z_count):
+        if i == half_groups:
+            x_arrivals(z_count - 1)
+        core_arrivals(group_at[i])
+        multiply(group_at[i], i == 0, i == z_count - 1)
+
+    cross.wait_send()
+    for i in range(half_groups):
+        int_copy(y * half_groups + i).wait_send()
+    for zz in range(z_count):
+        for h in range(2):
+
+            @pl.when(has_r & (zz <= z))
+            def _():
+                copy(RIGHT, zz, x, h).wait_send()
+
+            @pl.when(has_l & (zz >= z))
+            def _():
+                copy(LEFT, zz, x, h).wait_send()
+
+            copy(ACROSS, zz, x, h).wait_send()
+            copy(CORE, zz, x, h).wait_send()
+            copy(CORE2, zz, 1 - x, h).wait_send()
+
+    @pl.loop(0, occ_here // step)
+    def _(i):
+        cols = pl.ds(pl.multiple_of(i * step, step), step)
+        pltpu.make_async_copy(out_scr.at[cols, :], out_hbm.at[cols, :], out_sem.at[i]).wait()
+
+
+def relayed(amplitudes, amp_mask, integrals, int_mask, owner, occ_energy, vir_energy):
+    z_count = lax.axis_size("wide") // 4
+    k_total = amplitudes.shape[0] * lax.axis_size("wide") * 2
+    occ_here, vir_here = occ_energy.shape[0], integrals.shape[1]
+    vmem = pl.BlockSpec(memory_space=pltpu.VMEM)
+    smem = pl.BlockSpec(memory_space=pltpu.SMEM)
+    anywhere = pl.BlockSpec(memory_space=pl.ANY)
+    dma = pltpu.SemaphoreType.DMA
+    return pl.pallas_call(
+        functools.partial(ladder_kernel, z_count),
+        out_shape=jax.ShapeDtypeStruct((occ_here, vir_here), jnp.bfloat16),
+        in_specs=[anywhere, anywhere, vmem, vmem, smem, vmem, vmem],
+        out_specs=anywhere,
+        scratch_shapes=[
+            pltpu.VMEM((k_total, occ_here), jnp.bfloat16),
+            pltpu.VMEM((k_total, vir_here), jnp.bfloat16),
+            pltpu.VMEM((occ_here, vir_here), jnp.float32),
+            pltpu.VMEM((occ_here, vir_here), jnp.float32),
+            pltpu.VMEM((k_total // TILE, occ_here), jnp.float32),
+            pltpu.VMEM((k_total // TILE, vir_here), jnp.float32),
+            pltpu.VMEM((occ_here, vir_here), jnp.bfloat16),
+            pltpu.VMEM((occ_here, LANES), jnp.float32),
+            dma((2,)),
+            dma,
+            dma((z_count,)),
+            dma((z_count,)),
+            dma((5, 2 * z_count)),
+            dma((8 * z_count,)),
+            dma((occ_here // 256,)),
+        ],
+        compiler_params=pltpu.CompilerParams(
+            collective_id=0, has_side_effects=True, vmem_limit_bytes=40 * 2**20
+        ),
+        cost_estimate=pl.CostEstimate(
+            flops=2 * k_total * occ_here * vir_here, bytes_accessed=4 * 2**20, transcendentals=0
+        ),
+    )(
+        amplitudes,
+        integrals,
+        amp_mask,
+        int_mask,
+        owner,
+        occ_energy.reshape(-1, LANES),
+        vir_energy.reshape(-1, LANES),
+    )
+
+
+def fits(mesh, amplitudes, integrals):
+    wide, narrow = mesh.shape["wide"], mesh.shape["narrow"]
+    return (
+        narrow == 2
+        and wide % 8 == 0
+        and amplitudes.shape[0] == wide * narrow * TILE
+        and amplitudes.shape[1] % (2 * 1024) == 0
+        and (integrals.shape[1] // wide) % LANES == 0
+    )
+
+
 def solution(mesh):
-    return jax.shard_map(
-        shards,
-        mesh=mesh,
-        in_specs=(
-            P(("wide", "narrow"), None),
-            P(),
-            P("narrow", "wide"),
-            P(),
-            P(),
-            P("narrow"),
-            P(),
-        ),
-        out_specs=P("narrow", "wide"),
-        check_vma=False,
-    )
+    def run(amplitudes, amp_mask, integrals, int_mask, owner, occ_energy, vir_energy):
+        body = relayed if fits(mesh, amplitudes, integrals) else shards
+        return jax.shard_map(
+            body,
+            mesh=mesh,
+            in_specs=(
+                P(("wide", "narrow"), None),
+                P(),
+                P("narrow", "wide"),
+                P(),
+                P(),
+                P("narrow"),
+                P(),
+            ),
+            out_specs=P("narrow", "wide"),
+            check_vma=False,
+        )(amplitudes, amp_mask, integrals, int_mask, owner, occ_energy, vir_energy)
+
+    return run

time: 116 us -> 41.8 us (0.36)
  the two profiles are of different devices: /device:TPU:5 before, /device:TPU:16 now
where the time goes in v1:
time: 41.8 us; the launch traced here: 41.4 us
  Pallas kernels  34.7 us (83%)
  local copies, waits for them, and re-layouts  6.68 us (16%)
    pallas_call x1, Pallas kernels, relayed(): pl.pallas_call(functools.partial(ladder_kernel, z_count), out_shape=jax.S...  34.7 us
    unnamed x15, local copies, waits for them, and re-layouts  6.68 us

profile of v1, /device:TPU:16, one launch (start us, length us, event | category | flops | bytes accessed | tf_op | source)
XLA Modules:
  0.0 41.4 jit_solution(11101516134655067532)
XLA Ops:
  0.0 0.0 copy-start.6
  0.0 0.7 %copy-done.6 = s32[128]{0:T(128)S(1)} copy-done((s32[128]{0:T(128)S(1)}, s32[128]{0:T(128)}, u32[]{:S(2)}) %copy-start.6) | copy-done | bytes 536
  0.7 0.0 copy-start
  0.7 1.2 %copy-done = bf16[1024,512]{1,0:T(8,128)(2,1)S(1)} copy-done((bf16[1024,512]{1,0:T(8,128)(2,1)S(1)}, bf16[1024,512]{1,0:T(8,128)(2,1)}, u32[]{:S(2)}) %copy-start) | copy-done | bytes 1048600
  1.9 0.0 copy-start.1
  1.9 0.9 %copy-done.1 = bf16[64,2048]{1,0:T(8,128)(2,1)S(1)} copy-done((bf16[64,2048]{1,0:T(8,128)(2,1)S(1)}, bf16[64,2048]{1,0:T(8,128)(2,1)}, u32[]{:S(2)}) %copy-start.1) | copy-done | bytes 262168
  2.8 0.0 copy-start.2
  2.8 0.8 %copy-done.2 = f32[8192]{0:T(1024)S(1)} copy-done((f32[8192]{0:T(1024)S(1)}, f32[8192]{0:T(1024)}, u32[]{:S(2)}) %copy-start.2) | copy-done | bytes 32792
  3.6 0.0 copy-start.3
  3.6 0.7 %copy-done.3 = s32[32,32]{1,0:T(8,128)S(1)} copy-done((s32[32,32]{1,0:T(8,128)S(1)}, s32[32,32]{1,0:T(8,128)}, u32[]{:S(2)}) %copy-start.3) | copy-done | bytes 4120
  4.3 0.0 copy-start.4
  4.3 0.7 %copy-done.4 = s32[32,128]{1,0:T(8,128)S(1)} copy-done((s32[32,128]{1,0:T(8,128)S(1)}, s32[32,128]{1,0:T(8,128)}, u32[]{:S(2)}) %copy-start.4) | copy-done | bytes 16408
  5.0 0.0 copy-start.5
  5.0 0.7 %copy-done.5 = f32[1024]{0:T(1024)S(1)} copy-done((f32[1024]{0:T(1024)S(1)}, f32[1024]{0:T(1024)}, u32[]{:S(2)}) %copy-start.5) | copy-done | bytes 4120
  5.7 34.7 %shard_map.73 = bf16[1024,512]{1,0:T(8,128)(2,1)S(1)} custom-call(bf16[64,2048]{1,0:T(8,128)(2,1)S(1)} %copy-done.1, bf16[1024,512]{1,0:T(8,128)(2,1)S(1)} %copy-done, s32[32,32]{1,0:T(8,128)S(1)} %copy-done.3, s32[32,128]{1,0:T(8,128)S(1)} %copy-done.4, s32[128]{0:T(128)S(1)} %copy-done.6, f32[8,128]{1,0:T(8,128)S(1)} %bitcast.3, f32[64,128]{1,0:T(8,128)S(1)} %bitcast.2), custom_call_target="tpu_custom_call" | custom-call | flops 2147483648 | bytes 4194304 | tf_op jit(solution)/shard_map/pallas_call | solution.py:437
  40.4 1.0 %copy.9 = bf16[1024,512]{1,0:T(8,128)(2,1)} copy(bf16[1024,512]{1,0:T(8,128)(2,1)S(1)} %shard_map.73) | data formatting | bytes 2097152
Async XLA Ops:
  0.0 0.7 %copy-start.6 = (s32[128]{0:T(128)S(1)}, s32[128]{0:T(128)}, u32[]{:S(2)}) copy-start(s32[128]{0:T(128)} %owner_ref.1) | copy-start | bytes 1540
  0.7 1.2 %copy-start = (bf16[1024,512]{1,0:T(8,128)(2,1)S(1)}, bf16[1024,512]{1,0:T(8,128)(2,1)}, u32[]{:S(2)}) copy-start(bf16[1024,512]{1,0:T(8,128)(2,1)} %int_hbm.1) | copy-start | bytes 3145732
  1.9 0.9 %copy-start.1 = (bf16[64,2048]{1,0:T(8,128)(2,1)S(1)}, bf16[64,2048]{1,0:T(8,128)(2,1)}, u32[]{:S(2)}) copy-start(bf16[64,2048]{1,0:T(8,128)(2,1)} %amp_hbm.1) | copy-start | bytes 786436
  2.8 0.8 %copy-start.2 = (f32[8192]{0:T(1024)S(1)}, f32[8192]{0:T(1024)}, u32[]{:S(2)}) copy-start(f32[8192]{0:T(1024)} %param.13) | copy-start | bytes 98308
  3.6 0.7 %copy-start.3 = (s32[32,32]{1,0:T(8,128)S(1)}, s32[32,32]{1,0:T(8,128)}, u32[]{:S(2)}) copy-start(s32[32,32]{1,0:T(8,128)} %amask_ref.1) | copy-start | bytes 12292
  4.3 0.7 %copy-start.4 = (s32[32,128]{1,0:T(8,128)S(1)}, s32[32,128]{1,0:T(8,128)}, u32[]{:S(2)}) copy-start(s32[32,128]{1,0:T(8,128)} %imask_ref.1) | copy-start | bytes 49156
  5.0 0.7 %copy-start.5 = (f32[1024]{0:T(1024)S(1)}, f32[1024]{0:T(1024)}, u32[]{:S(2)}) copy-start(f32[1024]{0:T(1024)} %param.12) | copy-start | bytes 12292

commit v2 on v1

v2 whole, which is shorter than its diff:
```python
import functools

import jax
import jax.numpy as jnp
from jax import lax
from jax.experimental import pallas as pl
from jax.experimental.pallas import tpu as pltpu
from jax.sharding import PartitionSpec as P

TILE = 64


def contract_rows(summed, rows_in, int_part):
    return summed + lax.dot_general(
        rows_in, int_part, (((0,), (0,)), ((), ())), preferred_element_type=jnp.float32
    )


def contract_all(amp_full, int_full, starting):
    k_total = amp_full.shape[0]
    block_rows = min(512, k_total)
    summed = starting
    for first_row in range(0, k_total, block_rows):
        summed = contract_rows(
            summed,
            amp_full[first_row : first_row + block_rows],
            int_full[first_row : first_row + block_rows],
        )
    return summed


def shards(amplitudes, amp_mask, integrals, int_mask, owner, occ_energy, vir_energy):
    tile_width = TILE
    narrow_count = lax.axis_size("narrow")
    wide_index = lax.axis_index("wide")
    narrow_index = lax.axis_index("narrow")
    src_rows = amplitudes.shape[0]
    occ_all = amplitudes.shape[1]
    occ_here = occ_energy.shape[0]
    vir_here = integrals.shape[1]
    first_src = (wide_index * narrow_count + narrow_index) * src_rows
    src_tiles = (first_src + jnp.arange(src_rows, dtype=jnp.int32)) // tile_width
    src_mask = jnp.take(amp_mask, src_tiles, axis=0)
    src_wide = jnp.broadcast_to(
        src_mask[:, :, None], (src_rows, occ_all // tile_width, tile_width)
    ).reshape(src_rows, occ_all)
    masked = jnp.where(src_wide == 1, amplitudes, jnp.zeros((), amplitudes.dtype))
    vir_tiles_here = vir_here // tile_width
    slot_ids = wide_index * vir_tiles_here + jnp.arange(vir_tiles_here, dtype=jnp.int32)
    tile_ids = jnp.take(owner, slot_ids)
    vir_mask = jnp.take(int_mask, tile_ids, axis=1)
    int_rows = integrals.shape[0]
    row_tiles = int_rows // tile_width
    local_mask = lax.dynamic_slice_in_dim(vir_mask, narrow_index * row_tiles, row_tiles, 0)
    local_wide = jnp.broadcast_to(
        local_mask[:, None, :, None], (row_tiles, tile_width, vir_tiles_here, tile_width)
    ).reshape(int_rows, vir_here)
    int_masked = jnp.where(local_wide == 1, integrals, jnp.zeros((), integrals.dtype))
    int_full = lax.all_gather(int_masked, "narrow", axis=0, tiled=True)
    starting = jnp.zeros((occ_here, vir_here), jnp.float32)
    regrouped = lax.all_to_all(masked, "narrow", split_axis=1, concat_axis=0, tiled=True)
    amp_full = lax.all_gather(regrouped, "wide", axis=0, tiled=True)
    ladder = contract_all(amp_full, int_full, starting)
    vir_energy_here = jnp.take(vir_energy.reshape(-1, tile_width), tile_ids, axis=0).reshape(
        vir_here
    )
    denominator = vir_energy_here[None, :] - occ_energy[:, None]
    return (ladder / denominator).astype(jnp.bfloat16)


MESH = pl.DeviceIdType.MESH
LANES = 128


def lookup(table, z, y):
    value = jnp.int32(table[0][0])
    for zz in range(len(table)):
        for yy in range(2):
            if table[zz][yy] != table[0][0]:
                value = jnp.where((z == zz) & (y == yy), jnp.int32(table[zz][yy]), value)
    return value


ARRIVALS = (
    ("z", 0, 1, 3.5),
    ("x", 0, 0, 3.5),
    ("y", 1, 0, 5.5),
    ("z", 0, 2, 6.5),
    ("x", 0, 1, 6.5),
    ("z", 1, 1, 9.0),
    ("x", 1, 0, 9.0),
    ("z", 0, 3, 10.0),
    ("z", 1, 2, 12.0),
    ("x", 0, 2, 13.0),
    ("x", 1, 1, 14.5),
    ("z", 1, 3, 16.0),
    ("x", 0, 3, 17.0),
    ("x", 1, 2, 20.0),
    ("x", 1, 3, 23.0),
)


def schedule(z_count):
    half = z_count // 2
    event = {(kind, dist): i for i, (kind, cross, dist, _) in enumerate(ARRIVALS) if cross == 1}
    event["z", 0] = event["y", 0]
    chunks = [[None] * 2 for _ in range(z_count)]
    units = [[None] * 2 for _ in range(z_count)]
    place = [0] * (2 * z_count)
    for z in range(z_count):
        for y in range(2):
            groups = sorted(range(y * half, (y + 1) * half), key=lambda g: abs(g - z))
            chunks[z][y] = [(g, e) for g in groups for e in range(2)]
        for y in range(2):
            remote = chunks[z][1 - y]
            rows = []
            for g in range(z_count):
                for e in range(2):
                    at = event["xz"[1 - e], abs(g - z)]
                    n = remote.index((g, e)) if (g, e) in remote else -1
                    ready = max(ARRIVALS[at][3], 8.0 + 5.2 * n)
                    rows.append((ready, at, g, e, n))
            rows.sort()
            units[z][y] = rows
            for i, (ready, at, _, _, _) in enumerate(rows):
                late = [j for j, a in enumerate(ARRIVALS) if a[3] + 1.0 >= ready]
                place[i] = max(place[i], at, late[0] if late else len(ARRIVALS) - 1)
    for i in range(1, len(place)):
        place[i] = max(place[i], place[i - 1])
    return chunks, units, place


def ladder_kernel(
    z_count,
    amp_hbm,
    int_hbm,
    amask_hbm,
    imask_hbm,
    owner_hbm,
    occ_hbm,
    vir_hbm,
    out_ref,
    amp_scr,
    int_scr,
    acc,
    recip,
    amask,
    imask,
    occ_cols,
    amask_ref,
    imask_ref,
    owner_ref,
    occ_ref,
    vir_ref,
    own_sem,
    ycross_send,
    int_send,
    int_recv,
    send_sem,
    recv_sem,
):
    w = lax.axis_index("wide")
    y = lax.axis_index("narrow")
    z, x, c = w // 4, (w // 2) % 2, w % 2
    rows = amp_hbm.shape[0]
    occ_here, vir_here = acc.shape
    unit = int_scr.shape[0] // (2 * z_count)
    half_groups = z_count // 2
    chunks, units, place = schedule(z_count)

    def wide_id(zz, xx, cc):
        return zz * 4 + xx * 2 + cc

    y_peer = (w, 1 - y)
    x_peer = (wide_id(z, 1 - x, c), y)
    c_peer = (wide_id(z, x, 1 - c), y)
    r_peer = (w + 4, y)
    l_peer = (w - 4, y)
    has_r, has_l = z < z_count - 1, z > 0

    barrier = pltpu.get_barrier_semaphore()
    for peer in (y_peer, x_peer, c_peer):
        pl.semaphore_signal(barrier, inc=1, device_id=peer, device_id_type=MESH)

    @pl.when(has_r)
    def _():
        pl.semaphore_signal(barrier, inc=1, device_id=r_peer, device_id_type=MESH)

    @pl.when(has_l)
    def _():
        pl.semaphore_signal(barrier, inc=1, device_id=l_peer, device_id_type=MESH)

    small = [
        pltpu.make_async_copy(src, dst, own_sem.at[2 + i])
        for i, (src, dst) in enumerate(
            (
                (amask_hbm, amask_ref),
                (imask_hbm, imask_ref),
                (owner_hbm, owner_ref),
                (occ_hbm, occ_ref),
                (vir_hbm, vir_ref),
            )
        )
    ]
    for one in small:
        one.start()

    pl.semaphore_wait(barrier, 3 + jnp.where(has_r, 1, 0) + jnp.where(has_l, 1, 0))

    def block_id(zz, xx, cc, h):
        return wide_id(zz, xx, cc) * 2 + h

    def block(zz, xx, cc, h):
        first = pl.multiple_of(block_id(zz, xx, cc, h) * rows, rows)
        return amp_scr.at[pl.ds(first, rows), :]

    def half_cols(yy):
        return amp_hbm.at[:, pl.ds(pl.multiple_of(yy * occ_here, LANES), occ_here)]

    RIGHT, LEFT, ACROSS, CORE, CORE2 = range(5)
    peers = (r_peer, l_peer, x_peer, c_peer, c_peer)

    def copy(kind, zz, xx, h, src=None):
        there = block(zz, xx, c, h)
        return pltpu.make_async_remote_copy(
            src_ref=there if src is None else src,
            dst_ref=there,
            send_sem=send_sem.at[kind, zz * 2 + h],
            recv_sem=recv_sem.at[block_id(zz, xx, c, h)],
            device_id=peers[kind],
            device_id_type=MESH,
        )

    def arrived(zz, xx, cc, h):
        here = block(zz, xx, cc, h)
        pltpu.make_async_remote_copy(
            src_ref=here,
            dst_ref=here,
            send_sem=send_sem.at[CORE, zz * 2 + h],
            recv_sem=recv_sem.at[block_id(zz, xx, cc, h)],
            device_id=c_peer,
            device_id_type=MESH,
        ).wait_recv()

    cross = pltpu.make_async_remote_copy(
        src_ref=half_cols(1 - y),
        dst_ref=block(z, x, c, y),
        send_sem=ycross_send,
        recv_sem=recv_sem.at[block_id(z, x, c, y)],
        device_id=y_peer,
        device_id_type=MESH,
    )
    cross.start()

    def spread_own(h, src):
        @pl.when(has_r)
        def _():
            copy(RIGHT, z, x, h, src).start()

        @pl.when(has_l)
        def _():
            copy(LEFT, z, x, h, src).start()

        copy(ACROSS, z, x, h, src).start()
        copy(CORE, z, x, h, src).start()

    spread_own(y, half_cols(y))

    def unit_row(g, far):
        return (g * 2 + x + far - 2 * x * far) * unit

    def int_chunk(n):
        g = lookup([[r[n][0] for r in row] for row in chunks], z, y)
        first = unit_row(g, chunks[0][0][n][1])
        return pltpu.make_async_remote_copy(
            src_ref=int_hbm.at[
                pl.ds(pl.multiple_of(first - y * half_groups * 2 * unit, unit), unit), :
            ],
            dst_ref=int_scr.at[pl.ds(pl.multiple_of(first, unit), unit), :],
            send_sem=int_send.at[n],
            recv_sem=int_recv.at[n],
            device_id=y_peer,
            device_id_type=MESH,
        )

    n_chunks = 2 * half_groups
    int_chunk(0).start()

    own_copy = pltpu.make_async_copy(half_cols(y), block(z, x, c, y), own_sem.at[0])
    own_copy.start()
    kept = half_groups * 2 * unit
    held = pltpu.make_async_copy(
        int_hbm, int_scr.at[pl.ds(pl.multiple_of(y * kept, unit), kept), :], own_sem.at[1]
    )
    held.start()

    slots = vir_here // TILE

    def prepare_masks():
        for one in small:
            one.wait()
        lane = lax.broadcasted_iota(jnp.int32, (1, vir_here), 1) // TILE
        tile_of = jnp.zeros((1, vir_here), jnp.int32)
        for j in range(slots):
            tile_of = jnp.where(lane == j, owner_ref[w * slots + j], tile_of)
        q_tiles = imask_ref.shape[1]
        pick = lax.broadcasted_iota(jnp.int32, (q_tiles, vir_here), 0) == tile_of
        imask[...] = jnp.dot(
            imask_ref[...].astype(jnp.float32).astype(jnp.bfloat16),
            jnp.where(pick, 1.0, 0.0).astype(jnp.bfloat16),
            preferred_element_type=jnp.float32,
        )
        p_tiles = amask_ref.shape[1]
        p_lane = lax.broadcasted_iota(jnp.int32, (p_tiles, occ_here), 1) // TILE
        p_tile = y * (occ_here // TILE) + p_lane
        pick_p = lax.broadcasted_iota(jnp.int32, (p_tiles, occ_here), 0) == p_tile
        amask[...] = jnp.dot(
            amask_ref[...].astype(jnp.float32).astype(jnp.bfloat16),
            jnp.where(pick_p, 1.0, 0.0).astype(jnp.bfloat16),
            preferred_element_type=jnp.float32,
        )

    low = lax.broadcasted_iota(jnp.int32, (1, LANES), 1) < TILE

    def energies(tile, upper):
        row = vir_ref[pl.ds(tile // 2, 1), :]
        turned = jnp.concatenate([row[:, TILE:], row[:, :TILE]], axis=1)
        odd = jnp.full((1, LANES), tile % 2, jnp.int32) == upper
        return jnp.where(odd, row, turned)

    def prepare_reciprocals():
        occ_t = jnp.transpose(occ_ref[...])
        for j in range(occ_here // LANES):
            occ_cols[j * LANES : (j + 1) * LANES, :] = jnp.broadcast_to(
                occ_t[:, j : j + 1], (LANES, LANES)
            )
        for j in range(slots // 2):
            first = energies(owner_ref[w * slots + 2 * j], 0)
            second = energies(owner_ref[w * slots + 2 * j + 1], 1)
            vir_row = jnp.where(low, first, second)

            @pl.loop(0, occ_here // LANES)
            def _(i):
                at = pl.ds(pl.multiple_of(i * LANES, LANES), LANES)
                recip[at, j * LANES : (j + 1) * LANES] = 1.0 / (vir_row - occ_cols[at, :])

    step = 256

    def multiply(i):
        g = lookup([[r[i][2] for r in row] for row in units], z, y)
        far = lookup([[r[i][3] for r in row] for row in units], z, y)
        first_row = unit_row(g, far)
        xx = x + far - 2 * x * far
        for h in range(2):
            arrived(g, xx, 1 - c, h)

        order = [[r[i][4] for r in row] for row in units]
        here = int_scr.at[pl.ds(pl.multiple_of(first_row, unit), unit), :]
        for n in range(n_chunks):
            if any(n in row for row in order):

                @pl.when(lookup(order, z, y) == n)
                def _():
                    pltpu.make_async_remote_copy(
                        src_ref=here,
                        dst_ref=here,
                        send_sem=int_send.at[n],
                        recv_sem=int_recv.at[n],
                        device_id=y_peer,
                        device_id_type=MESH,
                    ).wait_recv()

        tiles = unit // TILE
        for t in range(tiles):
            at = pl.ds(pl.multiple_of(first_row + t * TILE, TILE), TILE)
            row = imask[pl.ds(first_row // TILE + t, 1), :].astype(jnp.bfloat16)
            int_scr[at, :] = int_scr[at, :] * jnp.broadcast_to(row, (TILE, vir_here))

        @pl.loop(0, occ_here // step)
        def _(p):
            cols = pl.ds(pl.multiple_of(p * step, step), step)
            parts = []
            for t in range(tiles):
                at = pl.ds(pl.multiple_of(first_row + t * TILE, TILE), TILE)
                row = amask[pl.ds(first_row // TILE + t, 1), cols].astype(jnp.bfloat16)
                parts.append(amp_scr[at, cols] * jnp.broadcast_to(row, (TILE, step)))
            left = jnp.concatenate(parts, axis=0)
            term = lax.dot_general(
                left,
                int_scr[pl.ds(pl.multiple_of(first_row, unit), unit), :],
                (((0,), (0,)), ((), ())),
                preferred_element_type=jnp.float32,
            )
            if i == 0:
                acc[cols, :] = term
            elif i < 2 * z_count - 1:
                acc[cols, :] += term
            else:
                out_ref[cols, :] = ((acc[cols, :] + term) * recip[cols, :]).astype(jnp.bfloat16)

    def each_side(dist, act):
        if dist == 0:
            act(z, None)
            return

        @pl.when(z - dist >= 0)
        def _():
            act(z - dist, RIGHT)

        @pl.when(z + dist <= z_count - 1)
        def _():
            act(z + dist, LEFT)

    def arrival(kind, h, dist):
        def from_z(zz, onward):
            arrived(zz, x, c, h)

            @pl.when(has_r if onward == RIGHT else has_l)
            def _():
                copy(onward, zz, x, h).start()

            copy(ACROSS, zz, x, h).start()
            copy(CORE, zz, x, h).start()

        def from_x(zz, _):
            arrived(zz, 1 - x, c, h)
            copy(CORE2, zz, 1 - x, h).start()

        if kind == "y":
            arrived(z, x, c, h)
            spread_own(h, block(z, x, c, h))
        else:
            each_side(dist, from_z if kind == "z" else from_x)

    sent = 1
    for at, (kind, crossed, dist, when) in enumerate(ARRIVALS):
        arrival(kind, 1 - y if crossed else y, dist)
        if at == 0:
            prepare_masks()
        if kind == "y":
            prepare_reciprocals()
        while sent < n_chunks and when >= 5.2 * (sent - 1) + 4.0:
            if sent >= 2:
                int_chunk(sent - 2).wait_send()
            int_chunk(sent).start()
            sent += 1
        for i in range(2 * z_count):
            if place[i] == at:
                if i == 0:
                    own_copy.wait()
                    held.wait()
                multiply(i)

    cross.wait_send()
    for n in range(n_chunks - 2, n_chunks):
        int_chunk(n).wait_send()
    for zz in range(z_count):
        for h in range(2):

            @pl.when(has_r & (zz <= z))
            def _():
                copy(RIGHT, zz, x, h).wait_send()

            @pl.when(has_l & (zz >= z))
            def _():
                copy(LEFT, zz, x, h).wait_send()

            copy(ACROSS, zz, x, h).wait_send()
            copy(CORE, zz, x, h).wait_send()
            copy(CORE2, zz, 1 - x, h).wait_send()


def relayed(amplitudes, amp_mask, integrals, int_mask, owner, occ_energy, vir_energy):
    z_count = lax.axis_size("wide") // 4
    k_total = amplitudes.shape[0] * lax.axis_size("wide") * 2
    occ_here, vir_here = occ_energy.shape[0], integrals.shape[1]
    hbm = pl.BlockSpec(memory_space=pltpu.HBM)
    dma = pltpu.SemaphoreType.DMA
    occ_rows, vir_rows = occ_here // LANES, vir_energy.shape[0] // LANES
    return pl.pallas_call(
        functools.partial(ladder_kernel, z_count),
        out_shape=jax.ShapeDtypeStruct((occ_here, vir_here), jnp.bfloat16),
        in_specs=[hbm] * 7,
        out_specs=pl.BlockSpec(memory_space=pltpu.VMEM),
        scratch_shapes=[
            pltpu.VMEM((k_total, occ_here), jnp.bfloat16),
            pltpu.VMEM((k_total, vir_here), jnp.bfloat16),
            pltpu.VMEM((occ_here, vir_here), jnp.float32),
            pltpu.VMEM((occ_here, vir_here), jnp.float32),
            pltpu.VMEM((k_total // TILE, occ_here), jnp.float32),
            pltpu.VMEM((k_total // TILE, vir_here), jnp.float32),
            pltpu.VMEM((occ_here, LANES), jnp.float32),
            pltpu.VMEM(amp_mask.shape, jnp.int32),
            pltpu.VMEM(int_mask.shape, jnp.int32),
            pltpu.SMEM(owner.shape, jnp.int32),
            pltpu.VMEM((occ_rows, LANES), jnp.float32),
            pltpu.VMEM((vir_rows, LANES), jnp.float32),
            dma((7,)),
            dma,
            dma((z_count,)),
            dma((z_count,)),
            dma((5, 2 * z_count)),
            dma((8 * z_count,)),
        ],
        compiler_params=pltpu.CompilerParams(
            collective_id=0, has_side_effects=True, vmem_limit_bytes=40 * 2**20
        ),
        cost_estimate=pl.CostEstimate(
            flops=2 * k_total * occ_here * vir_here, bytes_accessed=4 * 2**20, transcendentals=0
        ),
    )(
        amplitudes,
        integrals,
        amp_mask,
        int_mask,
        owner,
        occ_energy.reshape(-1, LANES),
        vir_energy.reshape(-1, LANES),
    )


def fits(mesh, amplitudes, integrals):
    wide, narrow = mesh.shape["wide"], mesh.shape["narrow"]
    return (
        narrow == 2
        and wide == 16
        and amplitudes.shape[0] == wide * narrow * TILE
        and amplitudes.shape[1] % (2 * 1024) == 0
        and (integrals.shape[1] // wide) % LANES == 0
    )


def solution(mesh):
    def run(amplitudes, amp_mask, integrals, int_mask, owner, occ_energy, vir_energy):
        body = relayed if fits(mesh, amplitudes, integrals) else shards
        return jax.shard_map(
            body,
            mesh=mesh,
            in_specs=(
                P(("wide", "narrow"), None),
                P(),
                P("narrow", "wide"),
                P(),
                P(),
                P("narrow"),
                P(),
            ),
            out_specs=P("narrow", "wide"),
            check_vma=False,
        )(amplitudes, amp_mask, integrals, int_mask, owner, occ_energy, vir_energy)

    return run
```

time: 41.8 us -> 41.2 us (0.986)
  the two profiles are of different devices: /device:TPU:16 before, /device:TPU:0 now
where the time goes in v2:
time: 41.2 us; the launch traced here: 40.8 us
  Pallas kernels  34.1 us (83%)
  local copies, waits for them, and re-layouts  6.68 us (16%)
    pallas_call x1, Pallas kernels, relayed(): pl.pallas_call(functools.partial(ladder_kernel, z_count), out_shape=jax.S...  34.1 us
    unnamed x15, local copies, waits for them, and re-layouts  6.68 us

profile of v2, /device:TPU:0, one launch (start us, length us, event | category | flops | bytes accessed | tf_op | source)
XLA Modules:
  0.0 40.8 jit_solution(4907563439907592163)
XLA Ops:
  0.0 0.0 copy-start.6
  0.0 0.7 %copy-done.6 = s32[128]{0:T(128)S(1)} copy-done((s32[128]{0:T(128)S(1)}, s32[128]{0:T(128)}, u32[]{:S(2)}) %copy-start.6) | copy-done | bytes 536
  0.7 0.0 copy-start
  0.7 1.2 %copy-done = bf16[1024,512]{1,0:T(8,128)(2,1)S(1)} copy-done((bf16[1024,512]{1,0:T(8,128)(2,1)S(1)}, bf16[1024,512]{1,0:T(8,128)(2,1)}, u32[]{:S(2)}) %copy-start) | copy-done | bytes 1048600
  1.9 0.0 copy-start.1
  1.9 0.9 %copy-done.1 = bf16[64,2048]{1,0:T(8,128)(2,1)S(1)} copy-done((bf16[64,2048]{1,0:T(8,128)(2,1)S(1)}, bf16[64,2048]{1,0:T(8,128)(2,1)}, u32[]{:S(2)}) %copy-start.1) | copy-done | bytes 262168
  2.8 0.0 copy-start.2
  2.8 0.8 %copy-done.2 = f32[8192]{0:T(1024)S(1)} copy-done((f32[8192]{0:T(1024)S(1)}, f32[8192]{0:T(1024)}, u32[]{:S(2)}) %copy-start.2) | copy-done | bytes 32792
  3.6 0.0 copy-start.3
  3.6 0.7 %copy-done.3 = s32[32,32]{1,0:T(8,128)S(1)} copy-done((s32[32,32]{1,0:T(8,128)S(1)}, s32[32,32]{1,0:T(8,128)}, u32[]{:S(2)}) %copy-start.3) | copy-done | bytes 4120
  4.3 0.0 copy-start.4
  4.3 0.7 %copy-done.4 = s32[32,128]{1,0:T(8,128)S(1)} copy-done((s32[32,128]{1,0:T(8,128)S(1)}, s32[32,128]{1,0:T(8,128)}, u32[]{:S(2)}) %copy-start.4) | copy-done | bytes 16408
  5.0 0.0 copy-start.5
  5.0 0.7 %copy-done.5 = f32[1024]{0:T(1024)S(1)} copy-done((f32[1024]{0:T(1024)S(1)}, f32[1024]{0:T(1024)}, u32[]{:S(2)}) %copy-start.5) | copy-done | bytes 4120
  5.7 34.1 %shard_map.73 = bf16[1024,512]{1,0:T(8,128)(2,1)S(1)} custom-call(bf16[64,2048]{1,0:T(8,128)(2,1)S(1)} %copy-done.1, bf16[1024,512]{1,0:T(8,128)(2,1)S(1)} %copy-done, s32[32,32]{1,0:T(8,128)S(1)} %copy-done.3, s32[32,128]{1,0:T(8,128)S(1)} %copy-done.4, s32[128]{0:T(128)S(1)} %copy-done.6, f32[8,128]{1,0:T(8,128)S(1)} %bitcast.3, f32[64,128]{1,0:T(8,128)S(1)} %bitcast.2), custom_call_target="tpu_custom_call" | custom-call | flops 2147483648 | bytes 4194304 | tf_op jit(solution)/shard_map/pallas_call | solution.py:480
  39.8 1.0 %copy.9 = bf16[1024,512]{1,0:T(8,128)(2,1)} copy(bf16[1024,512]{1,0:T(8,128)(2,1)S(1)} %shard_map.73) | data formatting | bytes 2097152
Async XLA Ops:
  0.0 0.7 %copy-start.6 = (s32[128]{0:T(128)S(1)}, s32[128]{0:T(128)}, u32[]{:S(2)}) copy-start(s32[128]{0:T(128)} %owner_hbm.1) | copy-start | bytes 1540
  0.7 1.2 %copy-start = (bf16[1024,512]{1,0:T(8,128)(2,1)S(1)}, bf16[1024,512]{1,0:T(8,128)(2,1)}, u32[]{:S(2)}) copy-start(bf16[1024,512]{1,0:T(8,128)(2,1)} %int_hbm.1) | copy-start | bytes 3145732
  1.9 0.9 %copy-start.1 = (bf16[64,2048]{1,0:T(8,128)(2,1)S(1)}, bf16[64,2048]{1,0:T(8,128)(2,1)}, u32[]{:S(2)}) copy-start(bf16[64,2048]{1,0:T(8,128)(2,1)} %amp_hbm.1) | copy-start | bytes 786436
  2.8 0.8 %copy-start.2 = (f32[8192]{0:T(1024)S(1)}, f32[8192]{0:T(1024)}, u32[]{:S(2)}) copy-start(f32[8192]{0:T(1024)} %param.13) | copy-start | bytes 98308
  3.6 0.7 %copy-start.3 = (s32[32,32]{1,0:T(8,128)S(1)}, s32[32,32]{1,0:T(8,128)}, u32[]{:S(2)}) copy-start(s32[32,32]{1,0:T(8,128)} %amask_hbm.1) | copy-start | bytes 12292
  4.3 0.7 %copy-start.4 = (s32[32,128]{1,0:T(8,128)S(1)}, s32[32,128]{1,0:T(8,128)}, u32[]{:S(2)}) copy-start(s32[32,128]{1,0:T(8,128)} %imask_hbm.1) | copy-start | bytes 49156
  5.0 0.7 %copy-start.5 = (f32[1024]{0:T(1024)S(1)}, f32[1024]{0:T(1024)}, u32[]{:S(2)}) copy-start(f32[1024]{0:T(1024)} %param.12) | copy-start | bytes 12292

commit v3 on v2

--- a/solution.py
+++ b/solution.py
@@ -139,7 +139,7 @@
     owner_hbm,
     occ_hbm,
     vir_hbm,
-    out_ref,
+    out_hbm,
     amp_scr,
     int_scr,
     acc,
@@ -152,6 +152,8 @@
     owner_ref,
     occ_ref,
     vir_ref,
+    out_scr,
+    out_sem,
     own_sem,
     ycross_send,
     int_send,
@@ -346,6 +348,10 @@
 
     step = 256
 
+    def out_copy(p):
+        cols = pl.ds(pl.multiple_of(p * step, step), step)
+        return pltpu.make_async_copy(out_scr.at[cols, :], out_hbm.at[cols, :], out_sem.at[p])
+
     def multiply(i):
         g = lookup([[r[i][2] for r in row] for row in units], z, y)
         far = lookup([[r[i][3] for r in row] for row in units], z, y)
@@ -396,7 +402,8 @@
             elif i < 2 * z_count - 1:
                 acc[cols, :] += term
             else:
-                out_ref[cols, :] = ((acc[cols, :] + term) * recip[cols, :]).astype(jnp.bfloat16)
+                out_scr[cols, :] = ((acc[cols, :] + term) * recip[cols, :]).astype(jnp.bfloat16)
+                out_copy(p).start()
 
     def each_side(dist, act):
         if dist == 0:
@@ -469,6 +476,10 @@
             copy(CORE, zz, x, h).wait_send()
             copy(CORE2, zz, 1 - x, h).wait_send()
 
+    @pl.loop(0, occ_here // step)
+    def _(p):
+        out_copy(p).wait()
+
 
 def relayed(amplitudes, amp_mask, integrals, int_mask, owner, occ_energy, vir_energy):
     z_count = lax.axis_size("wide") // 4
@@ -481,7 +492,7 @@
         functools.partial(ladder_kernel, z_count),
         out_shape=jax.ShapeDtypeStruct((occ_here, vir_here), jnp.bfloat16),
         in_specs=[hbm] * 7,
-        out_specs=pl.BlockSpec(memory_space=pltpu.VMEM),
+        out_specs=hbm,
         scratch_shapes=[
             pltpu.VMEM((k_total, occ_here), jnp.bfloat16),
             pltpu.VMEM((k_total, vir_here), jnp.bfloat16),
@@ -495,6 +506,8 @@
             pltpu.SMEM(owner.shape, jnp.int32),
             pltpu.VMEM((occ_rows, LANES), jnp.float32),
             pltpu.VMEM((vir_rows, LANES), jnp.float32),
+            pltpu.VMEM((occ_here, vir_here), jnp.bfloat16),
+            dma((occ_here // 256,)),
             dma((7,)),
             dma,
             dma((z_count,)),
@@ -503,7 +516,7 @@
             dma((8 * z_count,)),
         ],
         compiler_params=pltpu.CompilerParams(
-            collective_id=0, has_side_effects=True, vmem_limit_bytes=40 * 2**20
+            collective_id=0, has_side_effects=True, vmem_limit_bytes=60 * 2**20
         ),
         cost_estimate=pl.CostEstimate(
             flops=2 * k_total * occ_here * vir_here, bytes_accessed=4 * 2**20, transcendentals=0

time: 41.2 us -> 37.7 us (0.915)
  local copies, waits for them, and re-layouts: 6.68 us -> 2.26 us
  Pallas kernels: 34.1 us -> 35.3 us
    unnamed x15 -> x1, local copies, waits for them, and re-layouts: 6.68 us -> 2.26 us
    pallas_call x1, Pallas kernels: 34.1 us -> 35.3 us  [relayed(): pl.pallas_call(functools.partial(ladder_kernel, z_count), out_shape=jax.S...]
where the time goes in v3:
time: 37.7 us; the launch traced here: 37.6 us
  Pallas kernels  35.3 us (94%)
  local copies, waits for them, and re-layouts  2.26 us (6%)
    pallas_call x1, Pallas kernels, relayed(): pl.pallas_call(functools.partial(ladder_kernel, z_count), out_shape=jax.S...  35.3 us
    unnamed x1, local copies, waits for them, and re-layouts  2.26 us

profile of v3, /device:TPU:0, one launch (start us, length us, event | category | flops | bytes accessed | tf_op | source)
XLA Modules:
  0.0 37.6 jit_solution(16755498613601310511)
XLA Ops:
  0.0 35.3 %shard_map.73 = bf16[1024,512]{1,0:T(8,128)(2,1)} custom-call(bf16[64,2048]{1,0:T(8,128)(2,1)} %amp_hbm.1, bf16[1024,512]{1,0:T(8,128)(2,1)} %int_hbm.1, s32[32,32]{1,0:T(8,128)} %amask_hbm.1, s32[32,128]{1,0:T(8,128)} %imask_hbm.1, s32[128]{0:T(128)} %owner_hbm.1, f32[8,128]{1,0:T(8,128)} %bitcast.3, f32[64,128]{1,0:T(8,128)} %bitcast.2), custom_call_target="tpu_custom_call" | custom-call | flops 2147483648 | bytes 4194304 | tf_op jit(solution)/shard_map/pallas_call | solution.py:491
  35.3 2.3 %copy.9 = bf16[1024,512]{1,0:T(8,128)(2,1)} copy(bf16[1024,512]{1,0:T(8,128)(2,1)} %shard_map.73) | data formatting | bytes 2097152

commit v4 on v2

--- a/solution.py
+++ b/solution.py
@@ -86,17 +86,17 @@
     ("x", 0, 0, 3.5),
     ("y", 1, 0, 5.5),
     ("z", 0, 2, 6.5),
-    ("x", 0, 1, 6.5),
+    ("x", 0, 1, 7.0),
     ("z", 1, 1, 9.0),
-    ("x", 1, 0, 9.0),
+    ("x", 1, 0, 9.5),
     ("z", 0, 3, 10.0),
+    ("x", 0, 2, 11.0),
     ("z", 1, 2, 12.0),
-    ("x", 0, 2, 13.0),
     ("x", 1, 1, 14.5),
+    ("x", 0, 3, 15.0),
     ("z", 1, 3, 16.0),
-    ("x", 0, 3, 17.0),
-    ("x", 1, 2, 20.0),
-    ("x", 1, 3, 23.0),
+    ("x", 1, 2, 18.5),
+    ("x", 1, 3, 20.5),
 )
 
 
@@ -217,8 +217,8 @@
     def half_cols(yy):
         return amp_hbm.at[:, pl.ds(pl.multiple_of(yy * occ_here, LANES), occ_here)]
 
-    RIGHT, LEFT, ACROSS, CORE, CORE2 = range(5)
-    peers = (r_peer, l_peer, x_peer, c_peer, c_peer)
+    RIGHT, LEFT, ACROSS, CORE, CORE2, RIGHT2, LEFT2 = range(7)
+    peers = (r_peer, l_peer, x_peer, c_peer, c_peer, r_peer, l_peer)
 
     def copy(kind, zz, xx, h, src=None):
         there = block(zz, xx, c, h)
@@ -412,6 +412,11 @@
             act(z + dist, LEFT)
 
     def arrival(kind, h, dist):
+        along = h is own_half
+
+        def from_end(zz, onward):
+            return zz == (0 if onward == RIGHT else z_count - 1)
+
         def from_z(zz, onward):
             arrived(zz, x, c, h)
 
@@ -419,11 +424,23 @@
             def _():
                 copy(onward, zz, x, h).start()
 
-            copy(ACROSS, zz, x, h).start()
+            if along and dist >= 2:
+
+                @pl.when(jnp.logical_not(from_end(zz, onward)))
+                def _():
+                    copy(ACROSS, zz, x, h).start()
+            else:
+                copy(ACROSS, zz, x, h).start()
             copy(CORE, zz, x, h).start()
 
-        def from_x(zz, _):
+        def from_x(zz, onward):
             arrived(zz, 1 - x, c, h)
+            if along and 1 <= dist < z_count - 1:
+
+                @pl.when(from_end(zz, onward))
+                def _():
+                    copy(RIGHT2 if onward == RIGHT else LEFT2, zz, 1 - x, h).start()
+
             copy(CORE2, zz, 1 - x, h).start()
 
         if kind == "y":
@@ -432,9 +449,10 @@
         else:
             each_side(dist, from_z if kind == "z" else from_x)
 
+    own_half, other_half = y, 1 - y
     sent = 1
     for at, (kind, crossed, dist, when) in enumerate(ARRIVALS):
-        arrival(kind, 1 - y if crossed else y, dist)
+        arrival(kind, other_half if crossed else own_half, dist)
         if at == 0:
             prepare_masks()
         if kind == "y":
@@ -465,9 +483,26 @@
             def _():
                 copy(LEFT, zz, x, h).wait_send()
 
-            copy(ACROSS, zz, x, h).wait_send()
+            around = False
+            if zz == 0:
+                around = (h == own_half) & (z >= 2)
+            elif zz == z_count - 1:
+                around = (h == own_half) & (z <= z_count - 3)
+            if around is False:
+                copy(ACROSS, zz, x, h).wait_send()
+            else:
+
+                @pl.when(jnp.logical_not(around))
+                def _():
+                    copy(ACROSS, zz, x, h).wait_send()
+
             copy(CORE, zz, x, h).wait_send()
             copy(CORE2, zz, 1 - x, h).wait_send()
+
+    @pl.when(has_r & has_l)
+    def _():
+        copy(RIGHT2, 0, 1 - x, own_half).wait_send()
+        copy(LEFT2, z_count - 1, 1 - x, own_half).wait_send()
 
 
 def relayed(amplitudes, amp_mask, integrals, int_mask, owner, occ_energy, vir_energy):
@@ -499,7 +534,7 @@
             dma,
             dma((z_count,)),
             dma((z_count,)),
-            dma((5, 2 * z_count)),
+            dma((7, 2 * z_count)),
             dma((8 * z_count,)),
         ],
         compiler_params=pltpu.CompilerParams(
@@ -509,13 +544,18 @@
             flops=2 * k_total * occ_here * vir_here, bytes_accessed=4 * 2**20, transcendentals=0
         ),
     )(
-        amplitudes,
-        integrals,
-        amp_mask,
-        int_mask,
-        owner,
-        occ_energy.reshape(-1, LANES),
-        vir_energy.reshape(-1, LANES),
+        *(
+            pltpu.with_memory_space_constraint(one, pltpu.HBM)
+            for one in (
+                amplitudes,
+                integrals,
+                amp_mask,
+                int_mask,
+                owner,
+                occ_energy.reshape(-1, LANES),
+                vir_energy.reshape(-1, LANES),
+            )
+        )
     )
 
 

time: 41.2 us -> 35.5 us (0.86)
  the two profiles are of different devices: /device:TPU:0 before, /device:TPU:5 now
where the time goes in v4:
time: 35.5 us; the launch traced here: 35.4 us
  Pallas kernels  34.4 us (97%)
  local copies, waits for them, and re-layouts  0.97 us (3%)
    pallas_call x1, Pallas kernels, relayed(): pl.pallas_call(functools.partial(ladder_kernel, z_count), out_shape=jax.S...  34.4 us
    unnamed x1, local copies, waits for them, and re-layouts  0.97 us

profile of v4, /device:TPU:5, one launch (start us, length us, event | category | flops | bytes accessed | tf_op | source)
XLA Modules:
  0.0 35.4 jit_solution(13736345698579498863)
XLA Ops:
  0.0 34.4 %shard_map.73 = bf16[1024,512]{1,0:T(8,128)(2,1)S(1)} custom-call(bf16[64,2048]{1,0:T(8,128)(2,1)} %amp_hbm.1, bf16[1024,512]{1,0:T(8,128)(2,1)} %int_hbm.1, s32[32,32]{1,0:T(8,128)} %amask_hbm.1, s32[32,128]{1,0:T(8,128)} %imask_hbm.1, s32[128]{0:T(128)} %owner_hbm.1, f32[8,128]{1,0:T(8,128)} %bitcast.3, f32[64,128]{1,0:T(8,128)} %bitcast.2), custom_call_target="tpu_custom_call" | custom-call | flops 2147483648 | bytes 4194304 | tf_op jit(solution)/shard_map/pallas_call | solution.py:515
  34.4 1.0 %copy.9 = bf16[1024,512]{1,0:T(8,128)(2,1)} copy(bf16[1024,512]{1,0:T(8,128)(2,1)S(1)} %shard_map.73) | data formatting | bytes 2097152

commit v5 on v4

--- a/solution.py
+++ b/solution.py
@@ -90,11 +90,11 @@
     ("z", 1, 1, 9.0),
     ("x", 1, 0, 9.5),
     ("z", 0, 3, 10.0),
-    ("x", 0, 2, 11.0),
     ("z", 1, 2, 12.0),
+    ("x", 0, 2, 12.0),
     ("x", 1, 1, 14.5),
-    ("x", 0, 3, 15.0),
     ("z", 1, 3, 16.0),
+    ("x", 0, 3, 18.0),
     ("x", 1, 2, 18.5),
     ("x", 1, 3, 20.5),
 )
@@ -152,6 +152,7 @@
     owner_ref,
     occ_ref,
     vir_ref,
+    turned,
     own_sem,
     ycross_send,
     int_send,
@@ -284,7 +285,6 @@
         )
 
     n_chunks = 2 * half_groups
-    int_chunk(0).start()
 
     own_copy = pltpu.make_async_copy(half_cols(y), block(z, x, c, y), own_sem.at[0])
     own_copy.start()
@@ -324,9 +324,9 @@
 
     def energies(tile, upper):
         row = vir_ref[pl.ds(tile // 2, 1), :]
-        turned = jnp.concatenate([row[:, TILE:], row[:, :TILE]], axis=1)
+        swapped = jnp.concatenate([row[:, TILE:], row[:, :TILE]], axis=1)
         odd = jnp.full((1, LANES), tile % 2, jnp.int32) == upper
-        return jnp.where(odd, row, turned)
+        return jnp.where(odd, row, swapped)
 
     def prepare_reciprocals():
         occ_t = jnp.transpose(occ_ref[...])
@@ -354,6 +354,22 @@
         for h in range(2):
             arrived(g, xx, 1 - c, h)
 
+        tiles = unit // TILE
+        last = i == 2 * z_count - 1
+
+        def masked_amplitudes(cols):
+            parts = []
+            for t in range(tiles):
+                at = pl.ds(pl.multiple_of(first_row + t * TILE, TILE), TILE)
+                row = amask[pl.ds(first_row // TILE + t, 1), cols].astype(jnp.bfloat16)
+                parts.append(amp_scr[at, cols] * jnp.broadcast_to(row, (TILE, step)))
+            return jnp.concatenate(parts, axis=0)
+
+        if last:
+            for p in range(occ_here // step):
+                cols = pl.ds(p * step, step)
+                turned[cols, :] = jnp.transpose(masked_amplitudes(cols))
+
         order = [[r[i][4] for r in row] for row in units]
         here = int_scr.at[pl.ds(pl.multiple_of(first_row, unit), unit), :]
         for n in range(n_chunks):
@@ -370,33 +386,32 @@
                         device_id_type=MESH,
                     ).wait_recv()
 
-        tiles = unit // TILE
         for t in range(tiles):
             at = pl.ds(pl.multiple_of(first_row + t * TILE, TILE), TILE)
             row = imask[pl.ds(first_row // TILE + t, 1), :].astype(jnp.bfloat16)
             int_scr[at, :] = int_scr[at, :] * jnp.broadcast_to(row, (TILE, vir_here))
 
+        if last:
+            right = int_scr[pl.ds(pl.multiple_of(first_row, unit), unit), :]
+            for p in range(occ_here // step):
+                cols = pl.ds(p * step, step)
+                term = jnp.dot(turned[cols, :], right, preferred_element_type=jnp.float32)
+                out_ref[cols, :] = ((acc[cols, :] + term) * recip[cols, :]).astype(jnp.bfloat16)
+            return
+
         @pl.loop(0, occ_here // step)
         def _(p):
             cols = pl.ds(pl.multiple_of(p * step, step), step)
-            parts = []
-            for t in range(tiles):
-                at = pl.ds(pl.multiple_of(first_row + t * TILE, TILE), TILE)
-                row = amask[pl.ds(first_row // TILE + t, 1), cols].astype(jnp.bfloat16)
-                parts.append(amp_scr[at, cols] * jnp.broadcast_to(row, (TILE, step)))
-            left = jnp.concatenate(parts, axis=0)
             term = lax.dot_general(
-                left,
+                masked_amplitudes(cols),
                 int_scr[pl.ds(pl.multiple_of(first_row, unit), unit), :],
                 (((0,), (0,)), ((), ())),
                 preferred_element_type=jnp.float32,
             )
             if i == 0:
                 acc[cols, :] = term
-            elif i < 2 * z_count - 1:
+            else:
                 acc[cols, :] += term
-            else:
-                out_ref[cols, :] = ((acc[cols, :] + term) * recip[cols, :]).astype(jnp.bfloat16)
 
     def each_side(dist, act):
         if dist == 0:
@@ -450,11 +465,11 @@
             each_side(dist, from_z if kind == "z" else from_x)
 
     own_half, other_half = y, 1 - y
+    prepare_masks()
+    int_chunk(0).start()
     sent = 1
     for at, (kind, crossed, dist, when) in enumerate(ARRIVALS):
         arrival(kind, other_half if crossed else own_half, dist)
-        if at == 0:
-            prepare_masks()
         if kind == "y":
             prepare_reciprocals()
         while sent < n_chunks and when >= 5.2 * (sent - 1) + 4.0:
@@ -530,6 +545,7 @@
             pltpu.SMEM(owner.shape, jnp.int32),
             pltpu.VMEM((occ_rows, LANES), jnp.float32),
             pltpu.VMEM((vir_rows, LANES), jnp.float32),
+            pltpu.VMEM((occ_here, k_total // (2 * z_count)), jnp.bfloat16),
             dma((7,)),
             dma,
             dma((z_count,)),

time: 35.5 us -> 35.5 us (level)
  no operation moved by 1% of the time
where the time goes in v5:
time: 35.5 us; the launch traced here: 35.4 us
  Pallas kernels  34.4 us (97%)
  local copies, waits for them, and re-layouts  0.97 us (3%)
    pallas_call x1, Pallas kernels, relayed(): pl.pallas_call(functools.partial(ladder_kernel, z_count), out_shape=jax.S...  34.4 us
    unnamed x1, local copies, waits for them, and re-layouts  0.97 us

profile of v5, /device:TPU:5, one launch (start us, length us, event | category | flops | bytes accessed | tf_op | source)
XLA Modules:
  0.0 35.4 jit_solution(17739358221987945774)
XLA Ops:
  0.0 34.4 %shard_map.73 = bf16[1024,512]{1,0:T(8,128)(2,1)S(1)} custom-call(bf16[64,2048]{1,0:T(8,128)(2,1)} %amp_hbm.1, bf16[1024,512]{1,0:T(8,128)(2,1)} %int_hbm.1, s32[32,32]{1,0:T(8,128)} %amask_hbm.1, s32[32,128]{1,0:T(8,128)} %imask_hbm.1, s32[128]{0:T(128)} %owner_hbm.1, f32[8,128]{1,0:T(8,128)} %bitcast.3, f32[64,128]{1,0:T(8,128)} %bitcast.2), custom_call_target="tpu_custom_call" | custom-call | flops 2147483648 | bytes 4194304 | tf_op jit(solution)/shard_map/pallas_call | solution.py:530
  34.4 1.0 %copy.9 = bf16[1024,512]{1,0:T(8,128)(2,1)} copy(bf16[1024,512]{1,0:T(8,128)(2,1)S(1)} %shard_map.73) | data formatting | bytes 2097152

commit v6 on v5

--- a/solution.py
+++ b/solution.py
@@ -89,20 +89,21 @@
     ("x", 0, 1, 7.0),
     ("z", 1, 1, 9.0),
     ("x", 1, 0, 9.5),
-    ("z", 0, 3, 10.0),
     ("z", 1, 2, 12.0),
+    ("late", 0, 2, 12.0),
     ("x", 0, 2, 12.0),
+    ("z", 1, 3, 14.5),
     ("x", 1, 1, 14.5),
-    ("z", 1, 3, 16.0),
-    ("x", 0, 3, 18.0),
+    ("z", 0, 3, 17.0),
     ("x", 1, 2, 18.5),
-    ("x", 1, 3, 20.5),
+    ("x", 1, 3, 19.5),
+    ("x", 0, 3, 19.5),
 )
 
 
 def schedule(z_count):
     half = z_count // 2
-    event = {(kind, dist): i for i, (kind, cross, dist, _) in enumerate(ARRIVALS) if cross == 1}
+    event = {(kind, dist): i for i, (kind, _, dist, _) in enumerate(ARRIVALS)}
     event["z", 0] = event["y", 0]
     chunks = [[None] * 2 for _ in range(z_count)]
     units = [[None] * 2 for _ in range(z_count)]
@@ -432,12 +433,15 @@
         def from_end(zz, onward):
             return zz == (0 if onward == RIGHT else z_count - 1)
 
-        def from_z(zz, onward):
-            arrived(zz, x, c, h)
-
+        def hand_on(zz, onward):
             @pl.when(has_r if onward == RIGHT else has_l)
             def _():
                 copy(onward, zz, x, h).start()
+
+        def from_z(zz, onward):
+            arrived(zz, x, c, h)
+            if not (along and dist == 2):
+                hand_on(zz, onward)
 
             if along and dist >= 2:
 
@@ -462,7 +466,7 @@
             arrived(z, x, c, h)
             spread_own(h, block(z, x, c, h))
         else:
-            each_side(dist, from_z if kind == "z" else from_x)
+            each_side(dist, {"z": from_z, "late": hand_on, "x": from_x}[kind])
 
     own_half, other_half = y, 1 - y
     prepare_masks()

time: 35.5 us -> 36.6 us (1.031)
  Pallas kernels: 34.4 us -> 35.5 us
    pallas_call x1, Pallas kernels: 34.4 us -> 35.5 us  [relayed(): pl.pallas_call(functools.partial(ladder_kernel, z_count), out_shape=jax.S...]
where the time goes in v6:
time: 36.6 us; the launch traced here: 36.5 us
  Pallas kernels  35.5 us (97%)
  local copies, waits for them, and re-layouts  0.97 us (3%)
    pallas_call x1, Pallas kernels, relayed(): pl.pallas_call(functools.partial(ladder_kernel, z_count), out_shape=jax.S...  35.5 us
    unnamed x1, local copies, waits for them, and re-layouts  0.97 us

profile of v6, /device:TPU:5, one launch (start us, length us, event | category | flops | bytes accessed | tf_op | source)
XLA Modules:
  0.0 36.5 jit_solution(17266344789161884249)
XLA Ops:
  0.0 35.5 %shard_map.73 = bf16[1024,512]{1,0:T(8,128)(2,1)S(1)} custom-call(bf16[64,2048]{1,0:T(8,128)(2,1)} %amp_hbm.1, bf16[1024,512]{1,0:T(8,128)(2,1)} %int_hbm.1, s32[32,32]{1,0:T(8,128)} %amask_hbm.1, s32[32,128]{1,0:T(8,128)} %imask_hbm.1, s32[128]{0:T(128)} %owner_hbm.1, f32[8,128]{1,0:T(8,128)} %bitcast.3, f32[64,128]{1,0:T(8,128)} %bitcast.2), custom_call_target="tpu_custom_call" | custom-call | flops 2147483648 | bytes 4194304 | tf_op jit(solution)/shard_map/pallas_call | solution.py:534
  35.5 1.0 %copy.9 = bf16[1024,512]{1,0:T(8,128)(2,1)} copy(bf16[1024,512]{1,0:T(8,128)(2,1)S(1)} %shard_map.73) | data formatting | bytes 2097152

commit v7 on v5

--- a/solution.py
+++ b/solution.py
@@ -118,7 +118,7 @@
                 for e in range(2):
                     at = event["xz"[1 - e], abs(g - z)]
                     n = remote.index((g, e)) if (g, e) in remote else -1
-                    ready = max(ARRIVALS[at][3], 8.0 + 5.2 * n)
+                    ready = max(ARRIVALS[at][3], 9.5 + 5.6 * n)
                     rows.append((ready, at, g, e, n))
             rows.sort()
             units[z][y] = rows

time: 35.5 us -> 35.7 us (level)
  no operation moved by 1% of the time
where the time goes in v7:
time: 35.7 us; the launch traced here: 35.5 us
  Pallas kernels  34.6 us (97%)
  local copies, waits for them, and re-layouts  0.97 us (3%)
    pallas_call x1, Pallas kernels, relayed(): pl.pallas_call(functools.partial(ladder_kernel, z_count), out_shape=jax.S...  34.6 us
    unnamed x1, local copies, waits for them, and re-layouts  0.97 us

profile of v7, /device:TPU:5, one launch (start us, length us, event | category | flops | bytes accessed | tf_op | source)
XLA Modules:
  0.0 35.5 jit_solution(5183109662975498533)
XLA Ops:
  0.0 34.6 %shard_map.73 = bf16[1024,512]{1,0:T(8,128)(2,1)S(1)} custom-call(bf16[64,2048]{1,0:T(8,128)(2,1)} %amp_hbm.1, bf16[1024,512]{1,0:T(8,128)(2,1)} %int_hbm.1, s32[32,32]{1,0:T(8,128)} %amask_hbm.1, s32[32,128]{1,0:T(8,128)} %imask_hbm.1, s32[128]{0:T(128)} %owner_hbm.1, f32[8,128]{1,0:T(8,128)} %bitcast.3, f32[64,128]{1,0:T(8,128)} %bitcast.2), custom_call_target="tpu_custom_call" | custom-call | flops 2147483648 | bytes 4194304 | tf_op jit(solution)/shard_map/pallas_call | solution.py:530
  34.6 1.0 %copy.9 = bf16[1024,512]{1,0:T(8,128)(2,1)} copy(bf16[1024,512]{1,0:T(8,128)(2,1)S(1)} %shard_map.73) | data formatting | bytes 2097152
